TPU v7x, 32 devices: a whole 2x2x4 slice. The times are simulated.
32 devices in a mesh: feat: 8 (over y, x, core), node: 4 (over z).
Axes of the slice: x: 2, y: 2, z: 4, core: 2. Of those that a mesh axis runs over, the one named last changes fastest.
Arguments:
- features: bfloat16 [4, 512, 16384], P('node', 'feat'), may hold values from -6 to 6
- target_ids: int32 [4, 4096], P('node'), may hold values from 0 to 16383
- block_ids: int32 [4, 32, 8], P('node'), may hold values from 0 to 127
- tile_counts: int32 [4, 32], P('node'), may hold values from 1 to 8, as said below
- adjacency: bfloat16 [4, 32, 8, 128, 128], P('node'), may hold values from 0 to 0.25
- w_neigh: bfloat16 [256, 512], P(None, 'feat'), may hold values from -0.1875 to 0.1875
- w_self: bfloat16 [256, 512], P(None, 'feat'), may hold values from -0.1875 to 0.1875
- w_head: bfloat16 [256, 256], replicated, may hold values from -0.375 to 0.375
- grad_scores: bfloat16 [4, 4096, 256], P('node', 'feat'), may hold values from -6 to 6
Outputs:
- scores: bfloat16 [4, 4096, 256], P('node', 'feat')
- grad_head: float32 [256, 256], replicated
- grad_neigh: float32 [256, 512], P(None, 'feat')
- grad_self: float32 [256, 512], P(None, 'feat')
Inputs may be any that keep to these rules, and one draw needn't show every extreme that they name: `tile_counts`: one group, drawn from the seed, has all of its tiles at 8 live slots; every tile of the other groups has fewer than 8.
All inputs are finite; a program needn't handle non-finite values.
Results may differ from a plain program's by a relative error of at most 0.0056.
Values may be sent and summed in bfloat16 or wider, within the bound.
A program may use at most 64 MiB of HBM per device.

v0:
```python
import jax
import jax.numpy as jnp
from jax import lax
from jax.sharding import PartitionSpec as P


def aggregate_local(feature_rows, block_row, count_row, adjacency_group):
    width = feature_rows.shape[0]
    tiles = block_row.shape[0]
    slots = block_row.shape[1]
    blocks = feature_rows.reshape(width, -1, 128)
    gathered = jnp.take(blocks, block_row.reshape(-1), axis=1).reshape(width, tiles, slots, 128)
    live = (jnp.arange(slots, dtype=jnp.int32)[None, :] < count_row[:, None]).astype(jnp.bfloat16)
    masked = gathered * live[None, :, :, None]
    summed = jnp.einsum(
        "tkrs,ftks->ftr", adjacency_group, masked, preferred_element_type=jnp.float32
    )
    summed = summed / count_row.astype(jnp.float32)[None, :, None]
    return summed.astype(jnp.bfloat16).reshape(width, tiles * 128)


def contract_first(left, right):
    return lax.dot_general(
        left, right, (((0,), (1,)), ((), ())), preferred_element_type=jnp.float32
    )


def body(
    features, target_ids, block_ids, tile_counts, adjacency, w_neigh, w_self, w_head, grad_scores
):
    feature_rows = features[0]
    aggregate = aggregate_local(feature_rows, block_ids[0], tile_counts[0], adjacency[0])
    own = jnp.take(feature_rows, target_ids[0], axis=1)
    agg_part = aggregate
    own_part = own
    preact = lax.psum_scatter(
        contract_first(agg_part, w_neigh) + contract_first(own_part, w_self),
        "feat",
        scatter_dimension=0,
        tiled=True,
    )
    hidden = jax.nn.silu(preact).astype(jnp.bfloat16)
    scores = jnp.dot(hidden, w_head.T, preferred_element_type=jnp.float32).astype(jnp.bfloat16)
    cotangent = grad_scores[0]
    head_local = lax.dot_general(
        cotangent, hidden, (((0,), (0,)), ((), ())), preferred_element_type=jnp.float32
    )
    grad_head = lax.psum(head_local, ("feat", "node"))
    grad_hidden = jnp.dot(cotangent, w_head, preferred_element_type=jnp.float32)
    sigma = jax.nn.sigmoid(preact)
    grad_pre = (grad_hidden * sigma * (1.0 + preact * (1.0 - sigma))).astype(jnp.bfloat16)
    shard_piece = lax.all_gather(grad_pre, "feat", axis=0, tiled=True)
    agg_part = aggregate
    own_part = own
    neigh_local = contract_first(shard_piece, agg_part)
    self_local = contract_first(shard_piece, own_part)
    grad_neigh, grad_self = lax.psum((neigh_local, self_local), "node")
    return (scores[None], grad_head, grad_neigh, grad_self)


def solution(mesh):
    in_specs = (
        P("node", "feat", None),
        P("node", None),
        P("node", None, None),
        P("node", None),
        P("node", None, None, None, None),
        P(None, "feat"),
        P(None, "feat"),
        P(),
        P("node", "feat", None),
    )
    out_specs = (P("node", "feat", None), P(), P(None, "feat"), P(None, "feat"))
    return jax.shard_map(body, mesh=mesh, in_specs=in_specs, out_specs=out_specs, check_vma=False)
```

profile of v0, /device:TPU:0, one launch (start us, length us, event | category | flops | bytes accessed | tf_op | source)
XLA Modules:
  0.0 308.8 jit_solution(13335983999297234126)
XLA Ops:
  7.2 0.8 compare_and_fusion.1
  8.1 0.8 copy.23
  9.6 0.7 compare_select_fusion
  10.3 0.7 compare_and_fusion
  11.1 0.7 fusion.33
  11.9 4.8 %copy.26 = bf16[1,64,16384]{1,2,0:T(8,128)(2,1)} copy(bf16[1,64,16384]{2,1,0:T(8,128)(2,1)} %param.9) | data formatting | bytes 4194304 | tf_op args[0]
  17.3 1.4 copy.24
  18.6 3.1 gather_fusion
  21.7 13.8 %gather_fusion.1 = bf16[4096,64]{1,0:T(8,128)(2,1)S(1)} fusion(bf16[64,16384]{0,1:T(8,128)(2,1)} %bitcast.57, s32[4096]{0:T(1024)S(1)} %broadcast_clamp_fusion), kind=kCustom, calls=%fused_computation.1 | custom fusion | bytes 1064960 | tf_op jit(solution)/shard_map/jit(_take)/gather | solution.py:33
  35.5 1.5 fusion.29
  37.7 5.7 %fusion.19 = bf16[32,8,8,128]{3,2,1,0:T(8,128)(2,1)S(1)} fusion(bf16[1,32,8,128,128]{4,3,2,1,0:T(8,128)(2,1)} %param.13, bf16[64,32,8,128]{3,0,2,1:T(8,128)(2,1)S(1)} %bitcast.60, pred[32,8]{1,0:T(8,128)(4,1)S(1)} %copy.22, bf16[32,8]{1,0:T(8,128)(2,1)S(1)} %fusion.33, f32[32]{0:T(128)S(1)} %bitcast_convert_fusion), kind=kOutput, calls=%fused_computation.19 | convolution fusion | flops 541589504 | bytes 13108096 | tf_op jit(solution)/shard_map/tkrs,ftks->ftr/dot_general | solution.py:15
  43.4 2.7 convolution_add_fusion
  46.2 54.1 %reduce-scatter.2.cloned.1.call-done = f32[512,256]{1,0:T(8,128)} async-done(((f32[4096,256]{1,0:T(8,128)}), f32[512,256]{1,0:T(8,128)}) %reduce-scatter.2.cloned.1.call-update) | async-done | bytes 524304 | tf_op jit(solution)/shard_map/reduce_scatter | solution.py:36
  100.3 2.0 fusion.13
  102.4 2.1 convolution_bitcast_fusion
  104.6 26.3 %all-gather.2.cloned.1.call-done = bf16[4096,256]{1,0:T(8,128)(2,1)} async-done(((bf16[512,256]{1,0:T(8,128)(2,1)}), bf16[4096,256]{1,0:T(8,128)(2,1)}) %all-gather.2.cloned.1.call-update) | async-done | bytes 2097168 | tf_op jit(solution)/shard_map/all_gather | solution.py:52
  130.9 4.9 %fusion.30 = f32[256,64]{0,1:T(8,128)} fusion(bf16[4096,256]{1,0:T(8,128)(2,1)} %all-gather.2.cloned.1.call-done, bf16[4096,64]{1,0:T(8,128)(2,1)S(1)} %gather_fusion.1, pred[4096]{0:T(1024)(128)(4,1)S(1)} %compare_and_fusion), kind=kOutput, calls=%fused_computation.28 | convolution fusion | flops 134479872 | bytes 2691072 | tf_op jit(solution)/shard_map/dot_general | solution.py:23
  135.8 1.1 fusion.24
  136.9 1.0 fusion.14
  137.9 124.9 %all-reduce.4.cloned.1.call-done = f32[256,256]{0,1:T(8,128)} async-done(((f32[256,256]{0,1:T(8,128)}), f32[256,256]{0,1:T(8,128)}) %all-reduce.4.cloned.1.call-update) | async-done | bytes 262160 | tf_op jit(solution)/shard_map/psum | solution.py:48
  262.9 1.8 copy.27
  264.6 34.7 %all-reduce.6.cloned.1.call-done = (f32[256,64]{0,1:T(8,128)}, f32[256,64]{0,1:T(8,128)}) async-done(((f32[256,64]{0,1:T(8,128)}, f32[256,64]{0,1:T(8,128)}), (f32[256,64]{0,1:T(8,128)}, f32[256,64]{0,1:T(8,128)})) %all-reduce.6.cloned.1.call-update) | async-done | bytes 131088 | tf_op jit(solution)/shard_map/psum | solution.py:57
  299.4 1.5 copy.42
  300.8 1.5 copy.43
  (31 shorter events, 2.4 us)
Async XLA Ops:
  7.2 93.1 %copy-start = (bf16[1,512,256]{2,1,0:T(8,128)(2,1)S(1)}, bf16[1,512,256]{2,1,0:T(8,128)(2,1)}, u32[]{:S(2)}) copy-start(bf16[1,512,256]{2,1,0:T(8,128)(2,1)} %param.17) | copy-start | bytes 786436
  7.2 9.5 %copy-start.1 = (bf16[1,64,16384]{2,1,0:T(8,128)(2,1)S(1)}, bf16[1,64,16384]{2,1,0:T(8,128)(2,1)}, u32[]{:S(2)}) copy-start(bf16[1,64,16384]{2,1,0:T(8,128)(2,1)} %param.9) | copy-start | bytes 6291460
  7.2 93.1 %reduce-scatter.2.cloned.1.call-start = ((), (), s32[]{:S(2)}) async-start(), calls=%async_computation.1 | async-start | bytes 4718592 | tf_op jit(solution)/shard_map/reduce_scatter | solution.py:36
  21.7 13.8 %copy-start.4 = (bf16[256,64]{0,1:T(8,128)(2,1)S(1)}, bf16[256,64]{0,1:T(8,128)(2,1)}, u32[]{:S(2)}) copy-start(bf16[256,64]{0,1:T(8,128)(2,1)} %param.15) | copy-start | bytes 98308
  35.5 2.2 copy-start.2
  37.7 5.7 %copy-start.5 = (bf16[256,64]{0,1:T(8,128)(2,1)S(1)}, bf16[256,64]{0,1:T(8,128)(2,1)}, u32[]{:S(2)}) copy-start(bf16[256,64]{0,1:T(8,128)(2,1)} %param.14) | copy-start | bytes 98308
  46.1 54.2 %copy-start.7 = (bf16[256,256]{1,0:T(8,128)(2,1)S(1)}, bf16[256,256]{1,0:T(8,128)(2,1)}, u32[]{:S(2)}) copy-start(bf16[256,256]{1,0:T(8,128)(2,1)} %param.16) | copy-start | bytes 393220
  46.1 84.7 %all-gather.2.cloned.1.call-start = ((), (), s32[]{:S(2)}) async-start(), calls=%async_computation.3 | async-start | bytes 2359296 | tf_op jit(solution)/shard_map/all_gather | solution.py:52
  102.4 160.5 %all-reduce.4.cloned.1.call-start = ((), (), s32[]{:S(2)}) async-start(), calls=%async_computation.2 | async-start | bytes 524288 | tf_op jit(solution)/shard_map/psum | solution.py:48
  104.5 32.5 %copy-start.6 = (f32[512,256]{1,0:T(8,128)S(1)}, f32[512,256]{1,0:T(8,128)}, u32[]{:S(2)}) copy-start(f32[512,256]{1,0:T(8,128)} %reduce-scatter.2.cloned.1.call-done) | copy-start | bytes 1572868
  104.5 194.9 %all-reduce.6.cloned.1.call-start = ((), (), s32[]{:S(2)}) async-start(), calls=%async_computation.4 | async-start | bytes 262144 | tf_op jit(solution)/shard_map/psum | solution.py:57
  130.8 4.9 %copy-start.3 = (bf16[4096,256]{1,0:T(8,128)(2,1)S(1)}, bf16[4096,256]{1,0:T(8,128)(2,1)}, u32[]{:S(2)}) copy-start(bf16[4096,256]{1,0:T(8,128)(2,1)} %all-gather.2.cloned.1.call-done) | copy-start | bytes 6291460
Sparse Core Ops, SparseCore 0:
  46.2 53.9 reduce-scatter.1
  102.9 27.8 all-gather.1
  137.8 124.9 all-reduce.3
  265.8 33.5 all-reduce.5
where the time goes:
time: 309 us
  waiting for transfers between devices  240 us (78%)
  local copies, waits for them, and re-layouts  30 us (10%)
  matrix products  21 us (7%)
  between operations  13.9 us (4%)
  other arithmetic  3.71 us (1%)
    psum x1, waiting for transfers between devices, body(): grad_head = lax.psum(head_local, ('feat', 'node'))  125 us
    reduce_scatter x1, waiting for transfers between devices, body(): lax.psum_scatter(contract_first(agg_part, w_neigh) + contract_first(own_p...  54.1 us
    psum x1, waiting for transfers between devices, body(): grad_neigh, grad_self = lax.psum((neigh_local, self_local), 'node')  34.7 us
    all_gather x1, waiting for transfers between devices, body(): shard_piece = lax.all_gather(grad_pre, 'feat', axis=0, tiled=True)  26.3 us
    gather x1, local copies, waits for them, and re-layouts, body(): own = jnp.take(feature_rows, target_ids[0], axis=1)  13.8 us
    unnamed x22, local copies, waits for them, and re-layouts  11.6 us
    dot_general x4, matrix products, contract_first(): lax.dot_general(left, right, (((0,), (1,)), ((), ())), preferred_element_...  10.2 us
  transfers between devices with their start and end apart: 4, of which 4 were waited for; matrix products, arithmetic and copies ran while one was open for 4% of the time, Pallas kernels for 0%

commit v1 on v0

--- a/solution.py
+++ b/solution.py
@@ -45,7 +45,7 @@
     head_local = lax.dot_general(
         cotangent, hidden, (((0,), (0,)), ((), ())), preferred_element_type=jnp.float32
     )
-    grad_head = lax.psum(head_local, ("feat", "node"))
+    grad_head = lax.psum(lax.psum(head_local, "node"), "feat")
     grad_hidden = jnp.dot(cotangent, w_head, preferred_element_type=jnp.float32)
     sigma = jax.nn.sigmoid(preact)
     grad_pre = (grad_hidden * sigma * (1.0 + preact * (1.0 - sigma))).astype(jnp.bfloat16)

time: 309 us -> 242 us (0.78)
  waiting for transfers between devices: 240 us -> 173 us
    psum x2, waiting for transfers between devices: 160 us -> 92.2 us  [body(): grad_head = lax.psum(lax.psum(head_local, 'node'), 'feat')]
  transfers between devices with their start and end apart: 4 -> 4, of which waited for: 4 -> 4; matrix products, arithmetic and copies ran while one was open for 4% -> 1% of each run, Pallas kernels for 0% -> 0%
where the time goes in v1:
time: 242 us; the launch traced here: 241 us
  waiting for transfers between devices  173 us (71%)
  local copies, waits for them, and re-layouts  30 us (12%)
  matrix products  21 us (9%)
  between operations  13.9 us (6%)
  other arithmetic  3.71 us (2%)
    psum x2, waiting for transfers between devices, body(): grad_head = lax.psum(lax.psum(head_local, 'node'), 'feat')  92.2 us
    reduce_scatter x1, waiting for transfers between devices, body(): lax.psum_scatter(contract_first(agg_part, w_neigh) + contract_first(own_p...  54.1 us
    all_gather x1, waiting for transfers between devices, body(): shard_piece = lax.all_gather(grad_pre, 'feat', axis=0, tiled=True)  26.4 us
    gather x1, local copies, waits for them, and re-layouts, body(): own = jnp.take(feature_rows, target_ids[0], axis=1)  13.8 us
    unnamed x22, local copies, waits for them, and re-layouts  11.6 us
    dot_general x4, matrix products, contract_first(): lax.dot_general(left, right, (((0,), (1,)), ((), ())), preferred_element_...  10.2 us
    dot_general x1, matrix products, aggregate_local(): jnp.einsum('tkrs,ftks->ftr', adjacency_group, masked, preferred_element_t...  5.64 us
  transfers between devices with their start and end apart: 4, of which 4 were waited for; matrix products, arithmetic and copies ran while one was open for 1% of the time, Pallas kernels for 0%

profile of v1, /device:TPU:0, one launch (start us, length us, event | category | flops | bytes accessed | tf_op | source)
XLA Modules:
  0.0 241.5 jit_solution(7593313731821987894)
XLA Ops:
  7.2 0.8 compare_and_fusion.1
  8.1 0.8 copy.23
  9.6 0.7 compare_select_fusion
  10.3 0.7 compare_and_fusion
  11.1 0.7 fusion.33
  11.9 4.8 %copy.26 = bf16[1,64,16384]{1,2,0:T(8,128)(2,1)} copy(bf16[1,64,16384]{2,1,0:T(8,128)(2,1)} %param.9) | data formatting | bytes 4194304 | tf_op args[0]
  17.3 1.4 copy.24
  18.6 3.1 %gather_fusion = bf16[256,64,128]{2,1,0:T(8,128)(2,1)} fusion(bf16[64,128,128]{2,0,1:T(8,128)(2,1)S(1)} %copy.24, s32[1024]{0:T(1024)S(1)} %pad_clamp_fusion), kind=kCustom, calls=%fused_computation | custom fusion | bytes 8389632 | tf_op jit(solution)/shard_map/jit(_take)/gather | solution.py:12
  21.7 13.8 %gather_fusion.1 = bf16[4096,64]{1,0:T(8,128)(2,1)S(1)} fusion(bf16[64,16384]{0,1:T(8,128)(2,1)} %bitcast.57, s32[4096]{0:T(1024)S(1)} %broadcast_clamp_fusion), kind=kCustom, calls=%fused_computation.1 | custom fusion | bytes 1064960 | tf_op jit(solution)/shard_map/jit(_take)/gather | solution.py:33
  35.5 1.5 fusion.29
  37.7 5.6 %fusion.19 = bf16[32,8,8,128]{3,2,1,0:T(8,128)(2,1)S(1)} fusion(bf16[1,32,8,128,128]{4,3,2,1,0:T(8,128)(2,1)} %param.13, bf16[64,32,8,128]{3,0,2,1:T(8,128)(2,1)S(1)} %bitcast.60, pred[32,8]{1,0:T(8,128)(4,1)S(1)} %copy.22, bf16[32,8]{1,0:T(8,128)(2,1)S(1)} %fusion.33, f32[32]{0:T(128)S(1)} %bitcast_convert_fusion), kind=kOutput, calls=%fused_computation.19 | convolution fusion | flops 541589504 | bytes 13108096 | tf_op jit(solution)/shard_map/tkrs,ftks->ftr/dot_general | solution.py:15
  43.3 2.7 %convolution_add_fusion = f32[4096,256]{1,0:T(8,128)} fusion(f32[4096,256]{1,0:T(8,128)S(1)} %fusion.29, bf16[256,64]{0,1:T(8,128)(2,1)S(1)} %copy-done.5, bf16[32,8,8,128]{3,2,1,0:T(8,128)(2,1)S(1)} %fusion.19), kind=kOutput, calls=%fused_computation.4 | convolution fusion | flops 135266304 | bytes 8945664 | tf_op jit(solution)/shard_map/dot_general | solution.py:23
  46.1 54.1 %reduce-scatter.2.cloned.1.call-done = f32[512,256]{1,0:T(8,128)} async-done(((f32[4096,256]{1,0:T(8,128)}), f32[512,256]{1,0:T(8,128)}) %reduce-scatter.2.cloned.1.call-update) | async-done | bytes 524304 | tf_op jit(solution)/shard_map/reduce_scatter | solution.py:36
  100.2 2.0 fusion.13
  102.4 2.1 convolution_bitcast_fusion
  104.4 26.4 %all-gather.2.cloned.1.call-done = bf16[4096,256]{1,0:T(8,128)(2,1)} async-done(((bf16[512,256]{1,0:T(8,128)(2,1)}), bf16[4096,256]{1,0:T(8,128)(2,1)}) %all-gather.2.cloned.1.call-update) | async-done | bytes 2097168 | tf_op jit(solution)/shard_map/all_gather | solution.py:52
  130.8 4.9 %fusion.30 = f32[256,64]{0,1:T(8,128)} fusion(bf16[4096,256]{1,0:T(8,128)(2,1)} %all-gather.2.cloned.1.call-done, bf16[4096,64]{1,0:T(8,128)(2,1)S(1)} %gather_fusion.1, pred[4096]{0:T(1024)(128)(4,1)S(1)} %compare_and_fusion), kind=kOutput, calls=%fused_computation.28 | convolution fusion | flops 134479872 | bytes 2691072 | tf_op jit(solution)/shard_map/dot_general | solution.py:23
  135.7 1.1 fusion.24
  136.9 37.4 %all-reduce.6.cloned.1.call-done = (f32[256,256]{0,1:T(8,128)}, f32[256,64]{0,1:T(8,128)}, f32[256,64]{0,1:T(8,128)}) async-done(((f32[256,256]{0,1:T(8,128)}, f32[256,64]{0,1:T(8,128)}, f32[256,64]{0,1:T(8,128)}), (f32[256,256]{0,1:T(8,128)}, f32[256,64]{0,1:T(8,128)}, f32[256,64]{0,1:T(8,128)})) %all-reduce.6.cloned.1.call-update) | async-done | bytes 393232 | tf_op jit(solution)/shard_map/psum | solution.py:48
  174.3 1.0 fusion.14
  175.4 54.9 %all-reduce.4.cloned.1.call-done = f32[256,256]{0,1:T(8,128)} async-done(((f32[256,256]{0,1:T(8,128)}), f32[256,256]{0,1:T(8,128)}) %all-reduce.4.cloned.1.call-update) | async-done | bytes 262160 | tf_op jit(solution)/shard_map/psum | solution.py:48
  230.2 1.8 copy.27
  232.0 1.5 copy.43
  233.5 1.5 copy.44
  (31 shorter events, 2.4 us)
Async XLA Ops:
  7.2 93.1 %copy-start = (bf16[1,512,256]{2,1,0:T(8,128)(2,1)S(1)}, bf16[1,512,256]{2,1,0:T(8,128)(2,1)}, u32[]{:S(2)}) copy-start(bf16[1,512,256]{2,1,0:T(8,128)(2,1)} %param.17) | copy-start | bytes 786436
  7.2 9.5 %copy-start.1 = (bf16[1,64,16384]{2,1,0:T(8,128)(2,1)S(1)}, bf16[1,64,16384]{2,1,0:T(8,128)(2,1)}, u32[]{:S(2)}) copy-start(bf16[1,64,16384]{2,1,0:T(8,128)(2,1)} %param.9) | copy-start | bytes 6291460
  7.2 93.1 %reduce-scatter.2.cloned.1.call-start = ((), (), s32[]{:S(2)}) async-start(), calls=%async_computation.1 | async-start | bytes 4718592 | tf_op jit(solution)/shard_map/reduce_scatter | solution.py:36
  21.7 13.8 %copy-start.4 = (bf16[256,64]{0,1:T(8,128)(2,1)S(1)}, bf16[256,64]{0,1:T(8,128)(2,1)}, u32[]{:S(2)}) copy-start(bf16[256,64]{0,1:T(8,128)(2,1)} %param.15) | copy-start | bytes 98308
  35.5 2.2 copy-start.2
  37.7 5.7 %copy-start.5 = (bf16[256,64]{0,1:T(8,128)(2,1)S(1)}, bf16[256,64]{0,1:T(8,128)(2,1)}, u32[]{:S(2)}) copy-start(bf16[256,64]{0,1:T(8,128)(2,1)} %param.14) | copy-start | bytes 98308
  46.1 54.2 %copy-start.7 = (bf16[256,256]{1,0:T(8,128)(2,1)S(1)}, bf16[256,256]{1,0:T(8,128)(2,1)}, u32[]{:S(2)}) copy-start(bf16[256,256]{1,0:T(8,128)(2,1)} %param.16) | copy-start | bytes 393220
  46.1 84.7 %all-gather.2.cloned.1.call-start = ((), (), s32[]{:S(2)}) async-start(), calls=%async_computation.3 | async-start | bytes 2359296 | tf_op jit(solution)/shard_map/all_gather | solution.py:52
  102.3 72.0 %all-reduce.6.cloned.1.call-start = ((), (), s32[]{:S(2)}) async-start(), calls=%async_computation.4 | async-start | bytes 786432 | tf_op jit(solution)/shard_map/psum | solution.py:48
  104.4 69.9 %copy-start.6 = (f32[512,256]{1,0:T(8,128)S(1)}, f32[512,256]{1,0:T(8,128)}, u32[]{:S(2)}) copy-start(f32[512,256]{1,0:T(8,128)} %reduce-scatter.2.cloned.1.call-done) | copy-start | bytes 1572868
  130.8 4.9 %copy-start.3 = (bf16[4096,256]{1,0:T(8,128)(2,1)S(1)}, bf16[4096,256]{1,0:T(8,128)(2,1)}, u32[]{:S(2)}) copy-start(bf16[4096,256]{1,0:T(8,128)(2,1)} %all-gather.2.cloned.1.call-done) | copy-start | bytes 6291460
  136.9 93.3 %all-reduce.4.cloned.1.call-start = ((), (), s32[]{:S(2)}) async-start(), calls=%async_computation.2 | async-start | bytes 524288 | tf_op jit(solution)/shard_map/psum | solution.py:48
Sparse Core Ops, SparseCore 0:
  46.2 53.9 reduce-scatter.1
  102.9 27.8 all-gather.1
  137.0 37.2 all-reduce.5
  177.2 52.9 all-reduce.3
